TPU v7x, 32 devices: a whole 2x2x4 slice. The times are simulated.
32 devices in a mesh: col: 8 (over z, y), lev: 4 (over x, core).
Axes of the slice: x: 2, y: 2, z: 4, core: 2. Of those that a mesh axis runs over, the one named last changes fastest.
Arguments:
- fields: bfloat16 [2, 32, 8192], P(None, 'lev', 'col'), may hold values from 0.5 to 3
- bracket: int32 [8, 8192], P(None, 'col'), may hold values from 0 to 30
- fraction: float32 [8, 8192], P(None, 'col'), may hold values from 0 to 1
- remap_weights: bfloat16 [128, 128, 128], P('col'), may hold values from 0 to 0.015625
- intersections: int32 [3, 256], P(None, 'col'), may hold values from 0 to 63, as said below
- tile_owner: int32 [64], replicated, may hold values from 0 to 63, as said below
Outputs:
- normalized: float32 [2, 8, 64, 128], P(None, 'lev', 'col')
Inputs may be any that keep to these rules, and one draw needn't show every extreme that they name: `intersections`: row 0 names a source block of the entry's own col index; row 1 a target tile whose owner, tile_owner[tile] // 8, lies within 2 indices of the entry's col index or exactly 4 indices away, cyclically; row 2 a weight block of the entry's own col index. `tile_owner`: A permutation of the tiles.
All inputs are finite; a program needn't handle non-finite values.
Results may differ from a plain program's by a relative error of at most 0.00031.
Values may be sent and summed in bfloat16 or wider, within the bound.
A program may use at most 64 MiB of HBM per device.

v0:
```python
import jax
import jax.numpy as jnp
from jax import lax
from jax.sharding import PartitionSpec as P

F = 2
PLEV = 8
HALF = 2


epsilon = 1e-06


def passed_along(x, axis, by):
    size = lax.axis_size(axis)
    return lax.ppermute(x, axis, [(i, (i + by) % size) for i in range(size)])


def mix_levels(level_block, lower_level, weight_up):
    level_ids = jnp.arange(level_block.shape[1], dtype=jnp.int32)
    is_below = level_ids[None, :, None] == lower_level[:, None, :]
    is_above = level_ids[None, :, None] == lower_level[:, None, :] + 1
    level_coef = jnp.where(
        is_below, 1.0 - weight_up[:, None, :], jnp.where(is_above, weight_up[:, None, :], 0.0)
    )
    return jnp.sum(level_coef[None] * level_block.astype(jnp.float32)[:, None], axis=2)


def gather_rows(selector, partial_tiles):
    return lax.dot_general(
        selector,
        partial_tiles,
        (((0,), (0,)), ((), ())),
        precision=lax.Precision.HIGHEST,
        preferred_element_type=jnp.float32,
    )


def per_device(fields, bracket, fraction, remap_weights, intersections, tile_owner):
    lev_index = lax.axis_index("lev")
    plev_dev = PLEV // lax.axis_size("lev")
    column_levels = lax.all_gather(fields, "lev", axis=1, tiled=True)
    lower_level = lax.dynamic_slice_in_dim(bracket, lev_index * plev_dev, plev_dev, 0)
    weight_up = lax.dynamic_slice_in_dim(fraction, lev_index * plev_dev, plev_dev, 0)
    interp = mix_levels(column_levels, lower_level, weight_up).astype(jnp.bfloat16)
    block_cols = remap_weights.shape[1]
    tile_cells = remap_weights.shape[2]
    blocks = interp.reshape(F, plev_dev, -1, block_cols)
    chosen = jnp.take(blocks, intersections[0], axis=2)
    picked = jnp.take(remap_weights, intersections[2], axis=0)
    partial_tiles = jnp.einsum("fpeb,ebt->efpt", chosen, picked, preferred_element_type=jnp.float32)
    entries = partial_tiles.shape[0]
    partial_tiles = partial_tiles.reshape(entries, -1)
    tile_total = tile_owner.shape[0]
    col_count = lax.axis_size("col")
    tile_dev = tile_total // col_count
    matches = intersections[1][:, None] == jnp.arange(tile_total, dtype=jnp.int32)[None, :]
    slot_index = jnp.sum(jnp.where(matches, tile_owner[None, :], 0), axis=1)
    own_index = lax.axis_index("col")
    owner_dev = slot_index // tile_dev
    local_tile = slot_index % tile_dev
    offset_of = (owner_dev - own_index + HALF + col_count) % col_count - HALF
    local_hit = local_tile[:, None] == jnp.arange(tile_dev, dtype=jnp.int32)[None, :]
    remapped = jnp.zeros((tile_dev, partial_tiles.shape[1]), jnp.float32)
    offset_list = list(range(-HALF, HALF + 1)) + [col_count // 2]
    for offset in offset_list:
        selector = (local_hit & (offset_of == offset)[:, None]).astype(jnp.float32)
        outgoing = gather_rows(selector, partial_tiles)
        if offset == 0:
            remapped = remapped + outgoing
        else:
            remapped = remapped + passed_along(outgoing, "col", offset)
    remapped = remapped.reshape(tile_dev, F, plev_dev, tile_cells).transpose(1, 2, 0, 3)
    shifted_left = jnp.concatenate([remapped[..., :1], remapped[..., :-1]], axis=-1)
    shifted_right = jnp.concatenate([remapped[..., 1:], remapped[..., -1:]], axis=-1)
    filtered = 0.25 * shifted_left + 0.5 * remapped + 0.25 * shifted_right
    cells = float(tile_dev * tile_cells * col_count)
    local_sums = jnp.sum(filtered, axis=(2, 3))
    field_mean = lax.psum(local_sums, "col") / cells
    centered = filtered - field_mean[:, :, None, None]
    field_var = lax.psum(jnp.sum(centered * centered, axis=(2, 3)), "col") / cells
    return centered * lax.rsqrt(field_var + epsilon)[:, :, None, None]


def solution(mesh):
    in_specs = (
        P(None, "lev", "col"),
        P(None, "col"),
        P(None, "col"),
        P("col", None, None),
        P(None, "col"),
        P(),
    )
    out_specs = P(None, "lev", "col", None)
    return jax.shard_map(
        per_device, mesh=mesh, in_specs=in_specs, out_specs=out_specs, check_vma=False
    )
```

profile of v0, /device:TPU:0, one launch (start us, length us, event | category | flops | bytes accessed | tf_op | source)
XLA Modules:
  0.0 65.3 jit_solution(1566925330004750406)
XLA Ops:
  0.0 0.0 copy-start
  0.0 0.0 copy-start.2
  0.0 0.0 copy-start.1
  0.0 0.8 %fusion.43 = (s32[32]{0:T(128)S(1)}, s32[32]{0:T(128)S(1)}) fusion(s32[3,32]{1,0:T(4,128)} %param.10), kind=kLoop, calls=%fused_computation.70 | loop fusion | flops 192 | bytes 512 | tf_op jit(solution)/shard_map/jit(_take)/jit(_where)/select_n | solution.py:49
  0.8 0.0 copy-done.2
  0.8 0.8 %broadcast_subtract_fusion = (f32[2,1024]{1,0:T(2,128)S(1)}, f32[2,1024]{1,0:T(2,128)S(1)}) fusion(f32[8,1024]{1,0:T(8,128)} %param.8, s32[]{:T(128)S(6)} %select_n.125), kind=kLoop, calls=%fused_computation.52 | loop fusion | flops 2048 | bytes 24580 | tf_op jit(solution)/shard_map/sub | solution.py:24
  1.6 0.8 %broadcast_add_fusion = (s32[2,1024]{1,0:T(2,128)S(1)}, s32[2,1024]{1,0:T(2,128)S(1)}) fusion(s32[8,1024]{1,0:T(8,128)} %param.7, s32[]{:T(128)S(6)} %select_n.125), kind=kLoop, calls=%fused_computation.51 | loop fusion | flops 2048 | bytes 24580 | tf_op jit(solution)/shard_map/add | solution.py:22
  2.4 0.0 copy-done.1
  2.4 6.5 %all_gather.3 = bf16[2,32,1024]{2,1,0:T(8,128)(2,1)S(1)} all-gather(bf16[2,8,1024]{2,1,0:T(8,128)(2,1)S(1)} %copy-done.1), channel_id=1, replica_groups=mesh['col'=8,'lev'=4] {'lev'}, dimensions={1}, use_global_device_ids=true | all-gather | bytes 163840 | tf_op jit(solution)/shard_map/all_gather | solution.py:42
  8.9 0.0 copy-start.3
  8.9 0.6 copy-done.3
  9.5 0.2 select_reduce_fusion
  9.8 0.1 multiply_reduce_fusion
  9.9 0.6 gather_fusion
  10.5 0.0 copy-done
  10.5 0.7 %gather_fusion.1 = bf16[32,128,128]{2,1,0:T(8,128)(2,1)S(1)} fusion(bf16[16,128,128]{2,1,0:T(8,128)(2,1)S(1)} %copy-done, s32[1024]{0:T(1024)S(1)} %get-tuple-element.28), kind=kCustom, calls=%fused_computation.1 | custom fusion | bytes 2097280 | tf_op jit(solution)/shard_map/jit(_take)/gather | solution.py:50
  11.3 0.5 fusion
  11.7 0.1 reshape.156
  11.8 0.3 fusion.15
  12.1 4.0 %collective-permute-start = (f32[8,512]{1,0:T(8,128)S(1)}, f32[8,512]{1,0:T(8,128)S(1)}, u32[]{:S(2)}, u32[]{:S(2)}) collective-permute-start(f32[8,512]{1,0:T(8,128)S(1)} %fusion.15), channel_id=1, source_target_pairs={{0,24},{4,28},{8,0},{12,4},{16,8},{20,12},{24,16},{28,20},{1,25},{... | collective-permute-start | bytes 49160 | tf_op jit(solution)/shard_map/ppermute | solution.py:16
  16.1 0.3 fusion.17
  16.4 1.4 %collective-permute-start.1 = (f32[8,512]{1,0:T(8,128)S(1)}, f32[8,512]{1,0:T(8,128)S(1)}, u32[]{:S(2)}, u32[]{:S(2)}) collective-permute-start(f32[8,512]{1,0:T(8,128)S(1)} %fusion.17), channel_id=1, source_target_pairs={{0,28},{4,0},{8,4},{12,8},{16,12},{20,16},{24,20},{28,24},{1,29},{... | collective-permute-start | bytes 49160 | tf_op jit(solution)/shard_map/ppermute | solution.py:16
  17.8 0.3 fusion.23
  18.0 0.6 collective-permute-start.2
  18.7 0.3 fusion.25
  18.9 1.0 %collective-permute-start.3 = (f32[8,512]{1,0:T(8,128)S(1)}, f32[8,512]{1,0:T(8,128)S(1)}, u32[]{:S(2)}, u32[]{:S(2)}) collective-permute-start(f32[8,512]{1,0:T(8,128)S(1)} %fusion.25), channel_id=1, source_target_pairs={{0,8},{4,12},{8,16},{12,20},{16,24},{20,28},{24,0},{28,4},{1,9},{5... | collective-permute-start | bytes 49160 | tf_op jit(solution)/shard_map/ppermute | solution.py:16
  19.9 0.3 fusion.27
  20.1 0.1 collective-permute-start.4
  20.2 0.0 collective-permute-done
  20.2 0.0 collective-permute-done.1
  20.2 4.3 %collective-permute-done.2 = f32[8,512]{1,0:T(8,128)S(1)} collective-permute-done((f32[8,512]{1,0:T(8,128)S(1)}, f32[8,512]{1,0:T(8,128)S(1)}, u32[]{:S(2)}, u32[]{:S(2)}) %collective-permute-start.2) | collective-permute-done | bytes 16416 | tf_op jit(solution)/shard_map/ppermute | solution.py:16
  24.5 0.0 collective-permute-done.3
  24.5 0.4 collective-permute-done.4
  24.9 0.3 add_add_fusion
  25.2 0.1 fusion.49
  25.2 0.1 fusion.50
  25.3 0.2 fusion.46
  25.5 21.8 %psum.14 = f32[2,2]{1,0:T(2,128)S(1)} all-reduce(f32[2,2]{1,0:T(2,128)S(1)} %get-tuple-element.5), channel_id=1, replica_groups=mesh['col'=8,'lev'=4] {'col'}, use_global_device_ids=true, to_apply=%region_3.4 | all-reduce | flops 4 | bytes 32 | tf_op jit(solution)/shard_map/psum | solution.py:79
  47.3 0.2 multiply_reduce_fusion.1
  47.5 17.1 %psum.15 = f32[2,2]{1,0:T(2,128)S(1)} all-reduce(f32[2,2]{1,0:T(2,128)S(1)} %multiply_reduce_fusion.1), channel_id=1, replica_groups=mesh['col'=8,'lev'=4] {'col'}, use_global_device_ids=true, to_apply=%region_5.6 | all-reduce | flops 4 | bytes 32 | tf_op jit(solution)/shard_map/psum | solution.py:81
  64.6 0.7 %subtract_multiply_fusion = f32[2,2,8,128]{3,2,1,0:T(8,128)} fusion(f32[2,2,8,128]{3,2,1,0:T(8,128)S(1)} %get-tuple-element.6, f32[2,2]{1,0:T(2,128)S(1)} %add_rsqrt_fusion, f32[2,2]{1,0:T(2,128)S(1)} %broadcast_multiply_fusion), kind=kLoop, calls=%fused_computation.35 | loop fusion | flops 8192 | bytes 32800 | tf_op jit(solution)/shard_map/mul | solution.py:82
  (9 shorter events, 0.1 us)
Async XLA Ops:
  0.0 10.5 %copy-start = (bf16[16,128,128]{2,1,0:T(8,128)(2,1)S(1)}, bf16[16,128,128]{2,1,0:T(8,128)(2,1)}, u32[]{:S(2)}) copy-start(bf16[16,128,128]{2,1,0:T(8,128)(2,1)} %param.9) | copy-start | bytes 1572868
  0.0 0.8 %copy-start.2 = (s32[3,32]{1,0:T(4,128)S(1)}, s32[3,32]{1,0:T(4,128)}, u32[]{:S(2)}) copy-start(s32[3,32]{1,0:T(4,128)} %param.10) | copy-start | bytes 1156
  0.0 2.3 %copy-start.1 = (bf16[2,8,1024]{2,1,0:T(8,128)(2,1)S(1)}, bf16[2,8,1024]{2,1,0:T(8,128)(2,1)}, u32[]{:S(2)}) copy-start(bf16[2,8,1024]{2,1,0:T(8,128)(2,1)} %param.6) | copy-start | bytes 98308
  8.9 0.7 %copy-start.3 = (s32[64]{0:T(128)S(1)}, s32[64]{0:T(128)}, u32[]{:S(2)}) copy-start(s32[64]{0:T(128)} %param.11) | copy-start | bytes 772
  12.1 8.1 %collective-permute-start = (f32[8,512]{1,0:T(8,128)S(1)}, f32[8,512]{1,0:T(8,128)S(1)}, u32[]{:S(2)}, u32[]{:S(2)}) collective-permute-start(f32[8,512]{1,0:T(8,128)S(1)} %fusion.15), channel_id=1, source_target_pairs={{0,24},{4,28},{8,0},{12,4},{16,8},{20,12},{24,16},{28,20},{1,25},{... | collective-permute-start | bytes 49160 | tf_op jit(solution)/shard_map/ppermute | solution.py:16
  16.4 3.9 %collective-permute-start.1 = (f32[8,512]{1,0:T(8,128)S(1)}, f32[8,512]{1,0:T(8,128)S(1)}, u32[]{:S(2)}, u32[]{:S(2)}) collective-permute-start(f32[8,512]{1,0:T(8,128)S(1)} %fusion.17), channel_id=1, source_target_pairs={{0,28},{4,0},{8,4},{12,8},{16,12},{20,16},{24,20},{28,24},{1,29},{... | collective-permute-start | bytes 49160 | tf_op jit(solution)/shard_map/ppermute | solution.py:16
  18.0 6.4 %collective-permute-start.2 = (f32[8,512]{1,0:T(8,128)S(1)}, f32[8,512]{1,0:T(8,128)S(1)}, u32[]{:S(2)}, u32[]{:S(2)}) collective-permute-start(f32[8,512]{1,0:T(8,128)S(1)} %fusion.23), channel_id=1, source_target_pairs={{0,4},{4,8},{8,12},{12,16},{16,20},{20,24},{24,28},{28,0},{1,5},{5... | collective-permute-start | bytes 49160 | tf_op jit(solution)/shard_map/ppermute | solution.py:16
  18.9 5.6 %collective-permute-start.3 = (f32[8,512]{1,0:T(8,128)S(1)}, f32[8,512]{1,0:T(8,128)S(1)}, u32[]{:S(2)}, u32[]{:S(2)}) collective-permute-start(f32[8,512]{1,0:T(8,128)S(1)} %fusion.25), channel_id=1, source_target_pairs={{0,8},{4,12},{8,16},{12,20},{16,24},{20,28},{24,0},{28,4},{1,9},{5... | collective-permute-start | bytes 49160 | tf_op jit(solution)/shard_map/ppermute | solution.py:16
  20.1 4.8 %collective-permute-start.4 = (f32[8,512]{1,0:T(8,128)S(1)}, f32[8,512]{1,0:T(8,128)S(1)}, u32[]{:S(2)}, u32[]{:S(2)}) collective-permute-start(f32[8,512]{1,0:T(8,128)S(1)} %fusion.27), channel_id=1, source_target_pairs={{0,16},{4,20},{8,24},{12,28},{16,0},{20,4},{24,8},{28,12},{1,17},{... | collective-permute-start | bytes 49160 | tf_op jit(solution)/shard_map/ppermute | solution.py:16
where the time goes:
time: 65.6 us; the launch traced here: 65.3 us
  blocking collectives  45.4 us (69%)
  starting transfers between devices  7.09 us (11%)
  waiting for transfers between devices  4.7 us (7%)
  other arithmetic  3.75 us (6%)
  local copies, waits for them, and re-layouts  2.27 us (3%)
  matrix products  1.99 us (3%)
    psum x1, blocking collectives, per_device(): field_mean = lax.psum(local_sums, 'col') / cells  21.8 us
    psum x1, blocking collectives, per_device(): lax.psum(jnp.sum(centered * centered, axis=(2, 3)), 'col') / cells  17.1 us
    ppermute x5, starting transfers between devices, passed_along(): return lax.ppermute(x, axis, [(i, (i + by) % size) for i in range(size)])  7.09 us
    all_gather x1, blocking collectives, per_device(): column_levels = lax.all_gather(fields, 'lev', axis=1, tiled=True)  6.48 us
    ppermute x5, waiting for transfers between devices, passed_along(): return lax.ppermute(x, axis, [(i, (i + by) % size) for i in range(size)])  4.7 us
    dot_general x6, matrix products, gather_rows(): lax.dot_general(selector, partial_tiles, (((0,), (0,)), ((), ())), precis...  1.54 us
  transfers between devices with their start and end apart: 5, of which 2 were waited for; matrix products, arithmetic and copies ran while one was open for 2% of the time, Pallas kernels for 0%

commit v1 on v0

v1 whole, which is shorter than its diff:
```python
import functools

import jax
import jax.numpy as jnp
from jax import lax
from jax.experimental import pallas as pl
from jax.experimental.pallas import tpu as pltpu
from jax.sharding import PartitionSpec as P

HALF = 2
EPSILON = 1e-06


def offsets_of(n_col):
    near = [n_col // 2]
    for by in range(HALF, 0, -1):
        near += [by, -by]
    found = [0]
    for by in near:
        if by % n_col not in found:
            found.append(by % n_col)
    return found


def split3(x):
    high = x.astype(jnp.bfloat16)
    rest = x - high.astype(jnp.float32)
    mid = rest.astype(jnp.bfloat16)
    low = (rest - mid.astype(jnp.float32)).astype(jnp.bfloat16)
    return high, mid, low


def kernel(
    n_col, n_lev,
    fields_hbm, bracket_hbm, fraction_hbm, weights_hbm, inter_hbm, owner_hbm,
    out_ref,
    fields_v, bracket_v, fraction_v, weights_v, inter_v, owner_v,
    lev_out, lev_in, col_out, col_in, stats,
    local_sem, lev_send, lev_recv, col_send, col_recv, stat_send, stat_recv,
):
    F, lev_dev, cols = fields_v.shape
    plev = bracket_v.shape[0]
    plev_dev = plev // n_lev
    n_wb, blk, tile = weights_v.shape
    n_src = cols // blk
    n_ent = inter_v.shape[1]
    n_tiles = owner_v.shape[1]
    tile_dev = n_tiles // n_col
    offsets = offsets_of(n_col)
    me = lax.axis_index("col")
    lv = lax.axis_index("lev")

    barrier = pltpu.get_barrier_semaphore()
    for by in range(1, n_lev):
        pl.semaphore_signal(barrier, inc=1, device_id={"lev": lax.rem(lv + by, n_lev)}, device_id_type=pl.DeviceIdType.MESH)

    def greet(by, carry):
        pl.semaphore_signal(barrier, inc=1, device_id={"col": lax.rem(me + by, n_col)}, device_id_type=pl.DeviceIdType.MESH)
        return carry

    few = n_col <= 16
    lax.fori_loop(1, n_col, greet, 0, unroll=few)

    pairs = [(fields_hbm, fields_v), (bracket_hbm, bracket_v), (fraction_hbm, fraction_v),
             (inter_hbm, inter_v), (owner_hbm, owner_v), (weights_hbm, weights_v)]
    loads = [pltpu.make_async_copy(src, dst, local_sem.at[i]) for i, (src, dst) in enumerate(pairs)]
    for load in loads:
        load.start()

    for load in loads[:3]:
        load.wait()
    first = lv * lev_dev
    for s in range(n_src):
        here = slice(s * blk, (s + 1) * blk)
        lower = bracket_v[:, here] - first
        up = fraction_v[:, here]
        down = 1.0 - up
        sums = [None] * F
        values = [fields_v[f, :, here].astype(jnp.float32) for f in range(F)]
        for l in range(lev_dev):
            coef = jnp.where(lower == l, down, jnp.where(lower == l - 1, up, 0.0))
            for f in range(F):
                term = coef * values[f][l : l + 1, :]
                sums[f] = term if sums[f] is None else sums[f] + term
        for f in range(F):
            lev_out[:, f, s, :] = sums[f]

    pl.semaphore_wait(barrier, n_lev - 1 + n_col - 1)

    lev_copies = []
    for by in range(1, n_lev):
        to = lax.rem(lv + by, n_lev)
        lev_copies.append(pltpu.make_async_remote_copy(
            src_ref=lev_out.at[pl.ds(to * plev_dev, plev_dev)],
            dst_ref=lev_in.at[by - 1],
            send_sem=lev_send.at[by - 1],
            recv_sem=lev_recv.at[by - 1],
            device_id={"lev": to},
            device_id_type=pl.DeviceIdType.MESH,
        ))
    for copy in lev_copies:
        copy.start()

    loads[3].wait()
    loads[4].wait()
    rows = len(offsets) * tile_dev
    row = lax.broadcasted_iota(jnp.int32, (rows, n_tiles), 0)
    slot = jnp.zeros((rows, n_tiles), jnp.int32)
    for k, by in enumerate(offsets):
        base = lax.rem(me + by, n_col) * tile_dev - k * tile_dev
        slot = jnp.where((row >= k * tile_dev) & (row < (k + 1) * tile_dev), row + base, slot)
    one, nil = jnp.float32(1.0), jnp.float32(0.0)
    placed = jnp.where(slot == owner_v[...], one, nil).astype(jnp.bfloat16)
    tile_of = lax.broadcasted_iota(jnp.int32, (n_tiles, n_ent), 0) == inter_v[1:2, :]
    goes = jnp.dot(placed, jnp.where(tile_of, one, nil).astype(jnp.bfloat16), preferred_element_type=jnp.float32)
    pair_of = lax.broadcasted_iota(jnp.int32, (n_wb * n_src, n_ent), 0) == inter_v[2:3, :] * n_src + inter_v[0:1, :]
    counts = lax.dot_general(
        goes.astype(jnp.bfloat16), jnp.where(pair_of, one, nil).astype(jnp.bfloat16),
        (((1,), (1,)), ((), ())), preferred_element_type=jnp.float32,
    ).astype(jnp.bfloat16)
    counts = jnp.concatenate([counts] * 3, axis=1)
    loads[5].wait()

    interp = lev_out[pl.ds(lv * plev_dev, plev_dev)]
    for by, copy in enumerate(lev_copies):
        copy.wait_recv()
        interp = interp + lev_in[by]
    fp = plev_dev * F
    interp = interp.reshape(fp * n_src, blk).astype(jnp.bfloat16)
    products = []
    for w in range(n_wb):
        product = jnp.dot(interp, weights_v[w], preferred_element_type=jnp.float32)
        products.append(jnp.concatenate([product[i * n_src : (i + 1) * n_src] for i in range(fp)], axis=1))
    products = jnp.concatenate(split3(jnp.concatenate(products, axis=0)), axis=0)
    tiles = jnp.dot(counts, products, preferred_element_type=jnp.float32)
    for k in range(len(offsets)):
        col_out[k] = tiles[k * tile_dev : (k + 1) * tile_dev]
    col_copies = []
    for k in range(1, len(offsets)):
        col_copies.append(pltpu.make_async_remote_copy(
            src_ref=col_out.at[k],
            dst_ref=col_in.at[k - 1],
            send_sem=col_send.at[k - 1],
            recv_sem=col_recv.at[k - 1],
            device_id={"col": lax.rem(me + offsets[k], n_col)},
            device_id_type=pl.DeviceIdType.MESH,
        ))
        col_copies[-1].start()
    remapped = col_out[0]
    for k, copy in enumerate(col_copies):
        copy.wait_recv()
        remapped = remapped + col_in[k]

    lane = lax.broadcasted_iota(jnp.int32, (tile_dev, tile), 1)
    filtered = []
    for i in range(fp):
        x = remapped[:, i * tile : (i + 1) * tile]
        left = jnp.where(lane == 0, x, pltpu.roll(x, 1, 1))
        right = jnp.where(lane == tile - 1, x, pltpu.roll(x, tile - 1, 1))
        y = 0.25 * left + 0.5 * x + 0.25 * right
        filtered.append(y)
        total = jnp.sum(y, axis=0, keepdims=True)
        off = y - total * (1.0 / tile_dev)
        stats[0, i : i + 1, :] = total
        stats[0, fp + i : fp + i + 1, :] = jnp.sum(off * off, axis=0, keepdims=True)

    def stat_copy(by):
        return pltpu.make_async_remote_copy(
            src_ref=stats.at[0],
            dst_ref=stats.at[by],
            send_sem=stat_send.at[by],
            recv_sem=stat_recv.at[by],
            device_id={"col": lax.rem(me + by, n_col)},
            device_id_type=pl.DeviceIdType.MESH,
        )

    def send_stat(by, carry):
        stat_copy(by).start()
        return carry

    def take_stat(by, carry):
        stat_copy(by).wait_recv()
        return carry

    def end_stat(by, carry):
        stat_copy(by).wait_send()
        return carry

    lax.fori_loop(1, n_col, send_stat, 0, unroll=few)
    for copy in lev_copies + col_copies:
        copy.wait_send()
    lax.fori_loop(1, n_col, take_stat, 0, unroll=few)
    cells = 1.0 / float(tile_dev * tile * n_col)
    every = stats[...]
    sums = every[:, :fp]
    mean = jnp.sum(jnp.sum(sums, axis=0), axis=1, keepdims=True) * cells
    away = sums * (1.0 / tile_dev) - mean
    squares = jnp.sum(every[:, fp:], axis=0) + float(tile_dev) * jnp.sum(away * away, axis=0)
    scale = lax.rsqrt(jnp.sum(squares, axis=1, keepdims=True) * cells + EPSILON)
    for i in range(fp):
        p, f = divmod(i, F)
        out_ref[f, p] = (filtered[i] - mean[i : i + 1]) * scale[i : i + 1]
    lax.fori_loop(1, n_col, end_stat, 0, unroll=few)


def solution(mesh):
    n_col, n_lev = mesh.shape["col"], mesh.shape["lev"]

    def per_device(fields, bracket, fraction, remap_weights, intersections, tile_owner):
        F, lev_dev, cols = fields.shape
        plev = bracket.shape[0]
        plev_dev = plev // n_lev
        n_wb, blk, tile = remap_weights.shape
        n_src = cols // blk
        n_tiles = tile_owner.shape[0]
        tile_dev = n_tiles // n_col
        fp = plev_dev * F
        others = len(offsets_of(n_col)) - 1
        f32 = jnp.float32
        dma = pltpu.SemaphoreType.DMA
        return pl.pallas_call(
            functools.partial(kernel, n_col, n_lev),
            out_shape=jax.ShapeDtypeStruct((F, plev_dev, tile_dev, tile), f32),
            in_specs=[pl.BlockSpec(memory_space=pl.ANY)] * 6,
            out_specs=pl.BlockSpec(memory_space=pltpu.VMEM),
            scratch_shapes=[
                pltpu.VMEM(fields.shape, fields.dtype),
                pltpu.VMEM(bracket.shape, bracket.dtype),
                pltpu.VMEM(fraction.shape, fraction.dtype),
                pltpu.VMEM(remap_weights.shape, remap_weights.dtype),
                pltpu.VMEM(intersections.shape, intersections.dtype),
                pltpu.VMEM((1, n_tiles), tile_owner.dtype),
                pltpu.VMEM((plev, F, n_src, blk), f32),
                pltpu.VMEM((n_lev - 1, plev_dev, F, n_src, blk), f32),
                pltpu.VMEM((others + 1, tile_dev, fp * tile), f32),
                pltpu.VMEM((others, tile_dev, fp * tile), f32),
                pltpu.VMEM((n_col, 2 * fp, tile), f32),
                dma((6,)),
                dma((n_lev - 1,)),
                dma((n_lev - 1,)),
                dma((others,)),
                dma((others,)),
                dma((n_col,)),
                dma((n_col,)),
            ],
            compiler_params=pltpu.CompilerParams(collective_id=0, has_side_effects=True),
        )(fields, bracket, fraction, remap_weights, intersections, tile_owner.reshape(1, n_tiles))

    in_specs = (
        P(None, "lev", "col"),
        P(None, "col"),
        P(None, "col"),
        P("col", None, None),
        P(None, "col"),
        P(),
    )
    return jax.shard_map(
        per_device, mesh=mesh, in_specs=in_specs, out_specs=P(None, "lev", "col", None), check_vma=False
    )
```

time: 65.6 us -> 21.1 us (0.32)
  blocking collectives: 45.4 us -> 0 us
  Pallas kernels: 0 us -> 19.6 us
  starting transfers between devices: 7.09 us -> 0 us
  waiting for transfers between devices: 4.7 us -> 0 us
  other arithmetic: 3.75 us -> 0 us
  matrix products: 1.99 us -> 0 us
  local copies, waits for them, and re-layouts: 2.27 us -> 1.32 us
    psum x2 -> x0, blocking collectives: 38.9 us -> none  [the longest x1 21.8 us: per_device(): field_mean = lax.psum(local_sums, 'col') / cells]
    pallas_call x0 -> x1, Pallas kernels: none -> 19.6 us  [per_device(): pl.pallas_call(functools.partial(kernel, n_col, n_lev), out_shape=jax.Sha...]
    ppermute x5 -> x0, starting transfers between devices: 7.09 us -> none  [passed_along(): return lax.ppermute(x, axis, [(i, (i + by) % size) for i in range(size)])]
    all_gather x1 -> x0, blocking collectives: 6.48 us -> none  [per_device(): column_levels = lax.all_gather(fields, 'lev', axis=1, tiled=True)]
    ppermute x5 -> x0, waiting for transfers between devices: 4.7 us -> none  [passed_along(): return lax.ppermute(x, axis, [(i, (i + by) % size) for i in range(size)])]
    dot_general x7 -> x0, matrix products: 1.99 us -> none  [the longest x6 1.54 us: gather_rows(): lax.dot_general(selector, partial_tiles, (((0,), (0,)), ((), ())), precis...]
    gather x2 -> x0, local copies, waits for them, and re-layouts: 1.39 us -> none  [the longest x1 0.75 us: per_device(): picked = jnp.take(remap_weights, intersections[2], axis=0)]
    select_n x3 -> x0, other arithmetic: 0.84 us -> none  [the longest x1 0.79 us: per_device(): chosen = jnp.take(blocks, intersections[0], axis=2)]
  transfers between devices with their start and end apart: 5 -> 0, of which waited for: 2 -> 0; matrix products, arithmetic and copies ran while one was open for 2% -> 0% of each run, Pallas kernels for 0% -> 0%
where the time goes in v1:
time: 21.1 us; the launch traced here: 20.9 us
  Pallas kernels  19.6 us (93%)
  local copies, waits for them, and re-layouts  1.32 us (6%)
    pallas_call x1, Pallas kernels, per_device(): pl.pallas_call(functools.partial(kernel, n_col, n_lev), out_shape=jax.Sha...  19.6 us
    unnamed x1, local copies, waits for them, and re-layouts  1.32 us

profile of v1, /device:TPU:0, one launch (start us, length us, event | category | flops | bytes accessed | tf_op | source)
XLA Modules:
  0.0 20.9 jit_solution(12691089483498590657)
XLA Ops:
  0.0 19.6 %shard_map.64 = f32[2,2,8,128]{3,2,1,0:T(8,128)} custom-call(bf16[2,8,1024]{2,1,0:T(8,128)(2,1)} %fields_hbm.1, s32[8,1024]{1,0:T(8,128)} %bracket_hbm.1, f32[8,1024]{1,0:T(8,128)} %fraction_hbm.1, bf16[16,128,128]{2,1,0:T(8,128)(2,1)} %weights_hbm.1, s32[3,32]{1,0:T(4,128)} %inter_hbm.1, s32[1,64]{1,0:T(1,128)} %bitcast.1), custom_call_target="tpu_custom_call" | custom-call | tf_op jit(solution)/shard_map/pallas_call | solution.py:221
  19.6 1.3 %copy.8 = f32[2,2,8,128]{3,2,1,0:T(8,128)} copy(f32[2,2,8,128]{3,2,1,0:T(8,128)} %shard_map.64) | data formatting | bytes 32768

commit v2 on v1

--- a/solution.py
+++ b/solution.py
@@ -36,7 +36,7 @@
     out_ref,
     fields_v, bracket_v, fraction_v, weights_v, inter_v, owner_v,
     lev_out, lev_in, col_out, col_in, stats,
-    local_sem, lev_send, lev_recv, col_send, col_recv, stat_send, stat_recv,
+    local_sem, lev_send, lev_recv, col_send, col_recv, stat_send, stat_recv, relay,
 ):
     F, lev_dev, cols = fields_v.shape
     plev = bracket_v.shape[0]
@@ -54,12 +54,27 @@
     for by in range(1, n_lev):
         pl.semaphore_signal(barrier, inc=1, device_id={"lev": lax.rem(lv + by, n_lev)}, device_id_type=pl.DeviceIdType.MESH)
 
+    few = n_col <= 16 and n_col % 2 == 0
+    hops = n_col // 2
+
+    def tell(sem):
+        for there, to in (
+            (me >= 0, me + 1 - 2 * lax.rem(me, 2)), (me >= 2, me - 2), (me < n_col - 2, me + 2)
+        ):
+            @pl.when(there)
+            def _():
+                pl.semaphore_signal(sem, inc=1, device_id={"col": to}, device_id_type=pl.DeviceIdType.MESH)
+
     def greet(by, carry):
         pl.semaphore_signal(barrier, inc=1, device_id={"col": lax.rem(me + by, n_col)}, device_id_type=pl.DeviceIdType.MESH)
         return carry
 
-    few = n_col <= 16
-    lax.fori_loop(1, n_col, greet, 0, unroll=few)
+    if few:
+        greeted = 1 + jnp.where(me >= 2, 1, 0) + jnp.where(me < n_col - 2, 1, 0)
+        tell(barrier)
+    else:
+        greeted = n_col - 1
+        lax.fori_loop(1, n_col, greet, 0)
 
     pairs = [(fields_hbm, fields_v), (bracket_hbm, bracket_v), (fraction_hbm, fraction_v),
              (inter_hbm, inter_v), (owner_hbm, owner_v), (weights_hbm, weights_v)]
@@ -85,7 +100,7 @@
         for f in range(F):
             lev_out[:, f, s, :] = sums[f]
 
-    pl.semaphore_wait(barrier, n_lev - 1 + n_col - 1)
+    pl.semaphore_wait(barrier, n_lev - 1 + greeted)
 
     lev_copies = []
     for by in range(1, n_lev):
@@ -100,6 +115,8 @@
         ))
     for copy in lev_copies:
         copy.start()
+    if few and hops > 1:
+        tell(relay.at[0])
 
     loads[3].wait()
     loads[4].wait()
@@ -121,6 +138,11 @@
     counts = jnp.concatenate([counts] * 3, axis=1)
     loads[5].wait()
 
+    if few:
+        for hop in range(1, hops - 1):
+            pl.semaphore_wait(relay.at[hop - 1], greeted)
+            tell(relay.at[hop])
+
     interp = lev_out[pl.ds(lv * plev_dev, plev_dev)]
     for by, copy in enumerate(lev_copies):
         copy.wait_recv()
@@ -135,6 +157,8 @@
     tiles = jnp.dot(counts, products, preferred_element_type=jnp.float32)
     for k in range(len(offsets)):
         col_out[k] = tiles[k * tile_dev : (k + 1) * tile_dev]
+    if few and hops > 1:
+        pl.semaphore_wait(relay.at[hops - 2], greeted)
     col_copies = []
     for k in range(1, len(offsets)):
         col_copies.append(pltpu.make_async_remote_copy(
@@ -199,7 +223,8 @@
     scale = lax.rsqrt(jnp.sum(squares, axis=1, keepdims=True) * cells + EPSILON)
     for i in range(fp):
         p, f = divmod(i, F)
-        out_ref[f, p] = (filtered[i] - mean[i : i + 1]) * scale[i : i + 1]
+        at = (f * plev_dev + p) * tile_dev
+        out_ref[at : at + tile_dev] = (filtered[i] - mean[i : i + 1]) * scale[i : i + 1]
     lax.fori_loop(1, n_col, end_stat, 0, unroll=few)
 
 
@@ -220,7 +245,7 @@
         dma = pltpu.SemaphoreType.DMA
         return pl.pallas_call(
             functools.partial(kernel, n_col, n_lev),
-            out_shape=jax.ShapeDtypeStruct((F, plev_dev, tile_dev, tile), f32),
+            out_shape=pltpu.VMEM((F * plev_dev * tile_dev, tile), f32),
             in_specs=[pl.BlockSpec(memory_space=pl.ANY)] * 6,
             out_specs=pl.BlockSpec(memory_space=pltpu.VMEM),
             scratch_shapes=[
@@ -242,9 +267,10 @@
                 dma((others,)),
                 dma((n_col,)),
                 dma((n_col,)),
+                pltpu.SemaphoreType.REGULAR((max(n_col // 2 - 1, 1) if n_col <= 16 else 1,)),
             ],
             compiler_params=pltpu.CompilerParams(collective_id=0, has_side_effects=True),
-        )(fields, bracket, fraction, remap_weights, intersections, tile_owner.reshape(1, n_tiles))
+        )(fields, bracket, fraction, remap_weights, intersections, tile_owner.reshape(1, n_tiles)).reshape(F, plev_dev, tile_dev, tile)
 
     in_specs = (
         P(None, "lev", "col"),

time: 21.1 us -> 17.7 us (0.84)
  Pallas kernels: 19.6 us -> 16.9 us
  local copies, waits for them, and re-layouts: 1.32 us -> 0.61 us
    pallas_call x1, Pallas kernels: 19.6 us -> 16.9 us  [per_device(): pl.pallas_call(functools.partial(kernel, n_col, n_lev), out_shape=pltpu.V...]
    unnamed x1, local copies, waits for them, and re-layouts: 1.32 us -> 0.61 us
where the time goes in v2:
time: 17.7 us; the launch traced here: 17.6 us
  Pallas kernels  16.9 us (95%)
  local copies, waits for them, and re-layouts  0.61 us (3%)
    pallas_call x1, Pallas kernels, per_device(): pl.pallas_call(functools.partial(kernel, n_col, n_lev), out_shape=pltpu.V...  16.9 us
    unnamed x1, local copies, waits for them, and re-layouts  0.61 us

profile of v2, /device:TPU:0, one launch (start us, length us, event | category | flops | bytes accessed | tf_op | source)
XLA Modules:
  0.0 17.6 jit_solution(11154795338254323152)
XLA Ops:
  0.0 16.9 %shard_map.64 = f32[32,128]{1,0:T(8,128)S(1)} custom-call(bf16[2,8,1024]{2,1,0:T(8,128)(2,1)} %fields_hbm.1, s32[8,1024]{1,0:T(8,128)} %bracket_hbm.1, f32[8,1024]{1,0:T(8,128)} %fraction_hbm.1, bf16[16,128,128]{2,1,0:T(8,128)(2,1)} %weights_hbm.1, s32[3,32]{1,0:T(4,128)} %inter_hbm.1, s32[1,64]{1,0:T(1,128)} %bitcast.3), custom_call_target="tpu_custom_call" | custom-call | tf_op jit(solution)/shard_map/pallas_call | solution.py:246
  16.9 0.6 %copy.8 = f32[2,2,8,128]{3,2,1,0:T(8,128)} copy(f32[2,2,8,128]{3,2,1,0:T(8,128)S(1)} %bitcast.2) | data formatting | bytes 32768

commit v3 on v2

--- a/solution.py
+++ b/solution.py
@@ -12,9 +12,10 @@
 
 
 def offsets_of(n_col):
-    near = [n_col // 2]
-    for by in range(HALF, 0, -1):
+    near = []
+    for by in range(1, HALF + 1):
         near += [by, -by]
+    near.append(n_col // 2)
     found = [0]
     for by in near:
         if by % n_col not in found:
@@ -50,6 +51,12 @@
     me = lax.axis_index("col")
     lv = lax.axis_index("lev")
 
+    pairs = [(fields_hbm, fields_v), (bracket_hbm, bracket_v), (fraction_hbm, fraction_v),
+             (inter_hbm, inter_v), (owner_hbm, owner_v), (weights_hbm, weights_v)]
+    loads = [pltpu.make_async_copy(src, dst, local_sem.at[i]) for i, (src, dst) in enumerate(pairs)]
+    for load in loads[:3]:
+        load.start()
+
     barrier = pltpu.get_barrier_semaphore()
     for by in range(1, n_lev):
         pl.semaphore_signal(barrier, inc=1, device_id={"lev": lax.rem(lv + by, n_lev)}, device_id_type=pl.DeviceIdType.MESH)
@@ -76,10 +83,7 @@
         greeted = n_col - 1
         lax.fori_loop(1, n_col, greet, 0)
 
-    pairs = [(fields_hbm, fields_v), (bracket_hbm, bracket_v), (fraction_hbm, fraction_v),
-             (inter_hbm, inter_v), (owner_hbm, owner_v), (weights_hbm, weights_v)]
-    loads = [pltpu.make_async_copy(src, dst, local_sem.at[i]) for i, (src, dst) in enumerate(pairs)]
-    for load in loads:
+    for load in loads[3:]:
         load.start()
 
     for load in loads[:3]:
@@ -113,8 +117,8 @@
             device_id={"lev": to},
             device_id_type=pl.DeviceIdType.MESH,
         ))
-    for copy in lev_copies:
-        copy.start()
+    for by in sorted(range(1, n_lev), key=lambda by: -min(by, n_lev - by)):
+        lev_copies[by - 1].start()
     if few and hops > 1:
         tell(relay.at[0])
 

time: 17.7 us -> 17.5 us (0.989)
    pallas_call x1, Pallas kernels: 16.9 us -> 16.8 us  [per_device(): pl.pallas_call(functools.partial(kernel, n_col, n_lev), out_shape=pltpu.V...]
where the time goes in v3:
time: 17.5 us; the launch traced here: 17.4 us
  Pallas kernels  16.8 us (96%)
  local copies, waits for them, and re-layouts  0.61 us (3%)
    pallas_call x1, Pallas kernels, per_device(): pl.pallas_call(functools.partial(kernel, n_col, n_lev), out_shape=pltpu.V...  16.8 us
    unnamed x1, local copies, waits for them, and re-layouts  0.61 us

profile of v3, /device:TPU:0, one launch (start us, length us, event | category | flops | bytes accessed | tf_op | source)
XLA Modules:
  0.0 17.4 jit_solution(520204120039112475)
XLA Ops:
  0.0 16.8 %shard_map.64 = f32[32,128]{1,0:T(8,128)S(1)} custom-call(bf16[2,8,1024]{2,1,0:T(8,128)(2,1)} %fields_hbm.1, s32[8,1024]{1,0:T(8,128)} %bracket_hbm.1, f32[8,1024]{1,0:T(8,128)} %fraction_hbm.1, bf16[16,128,128]{2,1,0:T(8,128)(2,1)} %weights_hbm.1, s32[3,32]{1,0:T(4,128)} %inter_hbm.1, s32[1,64]{1,0:T(1,128)} %bitcast.3), custom_call_target="tpu_custom_call" | custom-call | tf_op jit(solution)/shard_map/pallas_call | solution.py:250
  16.8 0.6 %copy.8 = f32[2,2,8,128]{3,2,1,0:T(8,128)} copy(f32[2,2,8,128]{3,2,1,0:T(8,128)S(1)} %bitcast.2) | data formatting | bytes 32768
